TPU v7x, 256 devices: a whole 4x4x8 slice. The times are simulated.
256 devices in a mesh: dp: 32 (over y, x, core), expert: 8 (over z).
Axes of the slice: x: 4, y: 4, z: 8, core: 2. Of those that a mesh axis runs over, the one named last changes fastest.
Arguments:
- grads: bfloat16 [32, 64, 704, 1024], P('dp', 'expert'), may hold values from -1.1953125 to 1.1953125
- momentum: float32 [64, 704, 1024], P('expert', 'dp'), may hold values from -6 to 6
Outputs:
- momentum_out: float32 [64, 704, 1024], P('expert', 'dp')
- update: bfloat16 [64, 704, 1024], P('expert', 'dp')
All inputs are finite; a program needn't handle non-finite values.
Results may differ from a plain program's by a relative error of at most 0.04.
Values may be sent and summed in bfloat16 or wider, within the bound.
A program may use at most 128 MiB of HBM per device.

v0:
```python
import math

import jax
import jax.numpy as jnp
from jax import lax
from jax.sharding import PartitionSpec as P

ITERS = 3


coef_a = 3.4445
coef_b = -4.775
coef_c = 2.0315
beta_momentum = 0.95
norm_eps = 1e-07


def contract_rows(left, right):
    return lax.dot_general(
        left, right, (((1,), (1,)), ((), ())), preferred_element_type=jnp.float32
    )


def newton_schulz(matrix):
    rows_count, cols_count = matrix.shape
    values = matrix.astype(jnp.float32)
    total = jnp.sum(values * values)
    iterate = (values / (jnp.sqrt(total) + norm_eps)).astype(jnp.bfloat16)
    for turn in range(ITERS):
        gram_matrix = contract_rows(iterate, iterate).astype(jnp.bfloat16)
        squared = jnp.dot(gram_matrix, gram_matrix, preferred_element_type=jnp.float32)
        polynomial = (coef_b * gram_matrix.astype(jnp.float32) + coef_c * squared).astype(
            jnp.bfloat16
        )
        mixed = jnp.dot(polynomial, iterate, preferred_element_type=jnp.float32)
        iterate = (coef_a * iterate.astype(jnp.float32) + mixed).astype(jnp.bfloat16)
    factor = math.sqrt(max(rows_count, cols_count))
    return (iterate.astype(jnp.float32) * factor).astype(jnp.bfloat16)


def empty_update(matrix):
    return jnp.zeros_like(matrix)


def per_device(grads, momentum):
    dp_size = lax.axis_size("dp")
    my_dp = lax.axis_index("dp")
    my_group = lax.axis_index("expert")
    local_grads = grads[0]
    experts_here, hidden_rows, columns = local_grads.shape
    grad_sum = lax.psum_scatter(
        local_grads.astype(jnp.float32).astype(jnp.bfloat16), "dp", scatter_dimension=1, tiled=True
    ).astype(jnp.float32)
    momentum_out = beta_momentum * momentum + grad_sum
    blended = (grad_sum + beta_momentum * momentum_out).astype(jnp.bfloat16)
    owner_ids = (my_group * experts_here + jnp.arange(experts_here, dtype=jnp.int32)) % dp_size
    offset = (my_dp - my_group * experts_here) % dp_size
    is_owner = offset < experts_here
    owned_slot = jnp.minimum(offset, experts_here - 1)
    gathered = lax.all_gather(blended, "dp", axis=1, tiled=True)
    matrix = lax.dynamic_index_in_dim(gathered, owned_slot, 0, keepdims=False)
    orthogonal = lax.cond(is_owner, newton_schulz, empty_update, matrix)
    sending = orthogonal.reshape(dp_size, hidden_rows // dp_size, columns)
    returned = lax.all_to_all(sending, "dp", split_axis=0, concat_axis=0, tiled=True)
    update = jnp.take(returned, owner_ids, axis=0)
    return (momentum_out, update)


def solution(mesh):
    placed = (P("dp", "expert", None, None), P("expert", "dp", None))
    return jax.shard_map(
        per_device,
        mesh=mesh,
        in_specs=placed,
        out_specs=(P("expert", "dp", None), P("expert", "dp", None)),
        check_vma=False,
    )
```

profile of v0, /device:TPU:64, one launch (start us, length us, event | category | flops | bytes accessed | tf_op | source)
XLA Modules:
  0.0 284.6 jit_solution(5993052047434872262)
XLA Ops:
  7.2 0.0 reduce-scatter.2.cloned.1.call-start
  7.2 21.2 %copy.13 = bf16[1,8,704,1024]{3,1,2,0:T(8,128)(2,1)} copy(bf16[1,8,704,1024]{3,2,1,0:T(8,128)(2,1)} %param.4) | data formatting | bytes 23068672 | tf_op args[0]
  28.4 0.0 copy-start
  28.4 0.0 reduce-scatter.2.cloned.1.call-update
  28.5 0.0 all-gather.2.cloned.1.call-start
  28.5 110.8 %reduce-scatter.2.cloned.1.call-done = bf16[8,22,1024]{2,0,1:T(8,128)(2,1)} async-done(((bf16[8,704,1024]{2,0,1:T(8,128)(2,1)}), bf16[8,22,1024]{2,0,1:T(8,128)(2,1)}) %reduce-scatter.2.cloned.1.call-update) | async-done | bytes 360464 | tf_op jit(solution)/shard_map/reduce_scatter | solution.py:51
  139.4 0.0 copy-done
  139.4 2.1 fusion.11
  141.5 0.0 all-gather.2.cloned.1.call-update
  141.5 66.1 %all-gather.2.cloned.1.call-done = bf16[8,704,1024]{2,0,1:T(8,128)(2,1)} async-done(((bf16[8,22,1024]{2,0,1:T(8,128)(2,1)}), bf16[8,704,1024]{2,0,1:T(8,128)(2,1)}) %all-gather.2.cloned.1.call-update) | async-done | bytes 11534352 | tf_op jit(solution)/shard_map/all_gather | solution.py:60
  207.6 0.4 conditional.1
  207.6 0.2 broadcast.117
  208.0 1.4 reshape.69
  209.4 42.8 %all-to-all-start = ((bf16[32,22,1024]{2,1,0:T(8,128)(2,1)}), bf16[32,22,1024]{2,1,0:T(8,128)(2,1)S(1)}, u32[]{:S(2)}, u32[]{:S(2)}) async-start(bf16[32,22,1024]{2,1,0:T(8,128)(2,1)} %reshape.69), calls=%async_computation.1 | async-start | bytes 3145728 | tf_op jit(solution)/shard_map/all_to_all | solution.py:64
  252.3 23.9 %all-to-all-done = bf16[32,22,1024]{2,1,0:T(8,128)(2,1)S(1)} async-done(((bf16[32,22,1024]{2,1,0:T(8,128)(2,1)}), bf16[32,22,1024]{2,1,0:T(8,128)(2,1)S(1)}, u32[]{:S(2)}, u32[]{:S(2)}) %all-to-all-start) | async-done | bytes 1441824 | tf_op jit(solution)/shard_map/all_to_all | solution.py:64
  276.1 0.6 gather_fusion
  276.7 0.1 broadcast_select_fusion
  276.8 0.9 copy.11
  (3 shorter events, 0.0 us)
Async XLA Ops:
  7.2 132.2 %reduce-scatter.2.cloned.1.call-start = ((), (), s32[]{:S(2)}) async-start(), calls=%async_computation.2 | async-start | bytes 11894784 | tf_op jit(solution)/shard_map/reduce_scatter | solution.py:51
  28.4 110.9 %copy-start = (f32[8,22,1024]{2,0,1:T(8,128)S(1)}, f32[8,22,1024]{2,0,1:T(8,128)}, u32[]{:S(2)}) copy-start(f32[8,22,1024]{2,0,1:T(8,128)} %param.5) | copy-start | bytes 2162692
  28.5 179.2 %all-gather.2.cloned.1.call-start = ((), (), s32[]{:S(2)}) async-start(), calls=%async_computation.3 | async-start | bytes 11894784 | tf_op jit(solution)/shard_map/all_gather | solution.py:60
  209.4 66.8 %all-to-all-start = ((bf16[32,22,1024]{2,1,0:T(8,128)(2,1)}), bf16[32,22,1024]{2,1,0:T(8,128)(2,1)S(1)}, u32[]{:S(2)}, u32[]{:S(2)}) async-start(bf16[32,22,1024]{2,1,0:T(8,128)(2,1)} %reshape.69), calls=%async_computation.1 | async-start | bytes 3145728 | tf_op jit(solution)/shard_map/all_to_all | solution.py:64
Sparse Core Ops, SparseCore 0:
  28.6 110.7 reduce-scatter.1
  142.8 64.7 all-gather.1
where the time goes:
time: 285 us
  waiting for transfers between devices  201 us (71%)
  starting transfers between devices  42.9 us (15%)
  local copies, waits for them, and re-layouts  24.3 us (9%)
  between operations  14.1 us (5%)
    reduce_scatter x1, waiting for transfers between devices, per_device(): lax.psum_scatter(local_grads.astype(jnp.float32).astype(jnp.bfloat16), 'd...  111 us
    all_gather x1, waiting for transfers between devices, per_device(): gathered = lax.all_gather(blended, 'dp', axis=1, tiled=True)  66.1 us
    all_to_all x1, starting transfers between devices, per_device(): lax.all_to_all(sending, 'dp', split_axis=0, concat_axis=0, tiled=True)  42.8 us
    all_to_all x1, waiting for transfers between devices, per_device(): lax.all_to_all(sending, 'dp', split_axis=0, concat_axis=0, tiled=True)  23.9 us
    unnamed x4, local copies, waits for them, and re-layouts  22.2 us
  transfers between devices with their start and end apart: 3, of which 3 were waited for; matrix products, arithmetic and copies ran while one was open for 0% of the time, Pallas kernels for 0%

commit v1 on v0

v1 whole, which is shorter than its diff:
```python
import functools

import jax
import jax.numpy as jnp
from jax import lax
from jax.experimental import pallas as pl
from jax.experimental.pallas import tpu as pltpu
from jax.sharding import PartitionSpec as P

MESH = pl.DeviceIdType.MESH
ITERS = 3
A, B, C = 3.4445, -4.775, 2.0315
BETA = 0.95
EPS = 1e-07

SIDE = 4
CHIPS = SIDE * SIDE
EXPERTS = 8
MINE = 4
HID, D = 704, 1024
ROWS = HID // CHIPS
SLOT = 48
HELD = 720
OWN = HID // (2 * CHIPS)
ROUNDS = 4
W = D // ROUNDS
TALL = CHIPS * SLOT
LANES = 128
STEP = 192


def kernel(grads, mom, mo_out, up_out, own, got, stage, r1, r2, p2, r3, bl, mm, mo,
           xa, xb, gb, up, own_s, die_ss, die_rs, s1_s, s1_r, s2_s, s2_r, h_s, h_r,
           p_s, p_r, g_s, g_r, m_l, m_s, m_r, mo_l, mo_s, mo_r, u_s, u_r):
    me = lax.axis_index("dp")
    z = lax.axis_index("expert")
    c = me % 2
    x = (me // 2) % SIDE
    y = me // (2 * SIDE)
    a = jnp.where(c == 0, x, y)
    b = jnp.where(c == 0, y, x)

    def at(a_, b_):
        a_, b_ = a_ % SIDE, b_ % SIDE
        row = jnp.where(c == 0, b_, a_)
        col = jnp.where(c == 0, a_, b_)
        return ((row * SIDE + col) * 2 + c, z)

    sib = (me + 1 - 2 * c, z)
    an, ap = at(a + 1, b), at(a + 3, b)
    bn, bp, bo = at(a, b + 1), at(a, b + 3), at(a, b + 2)
    a1, a2, a3 = (a + 1) % SIDE, (a + 2) % SIDE, (a + 3) % SIDE
    b1, b2, b3 = (b + 1) % SIDE, (b + 2) % SIDE, (b + 3) % SIDE

    def remote(src, dst, ss, rs, dev):
        return pltpu.make_async_remote_copy(
            src, dst, ss, rs, device_id=dev, device_id_type=MESH)

    barrier = pltpu.get_barrier_semaphore()
    for dev in (sib, an, ap, bn, bp, bo):
        pl.semaphore_signal(barrier, inc=1, device_id=dev, device_id_type=MESH)
    pl.semaphore_wait(barrier, 6)

    def cols(q):
        return pl.ds(q * W, W)

    def die(q):
        return remote(
            grads.at[pl.ds(MINE * (1 - c), MINE), :, cols(q)],
            got.at[q, :, pl.ds(0, HID), :], die_ss.at[q], die_rs.at[q], sib)

    def load(q):
        return pltpu.make_async_copy(
            grads.at[pl.ds(MINE * c, MINE), :, cols(q)],
            own.at[q, :, pl.ds(0, HID), :], own_s.at[q])

    die(0).start()
    load(0).start()
    die(1).start()
    load(1).start()
    held = pl.ds(pl.multiple_of(OWN * EXPERTS * c, 8), OWN * EXPERTS)
    my_m = [pltpu.make_async_copy(
        mom.at[:, pl.ds(LANES * n, LANES)], mm.at[n, held], m_l.at[n]) for n in range(D // LANES)]
    his_m = [remote(mom.at[:, pl.ds(LANES * n, LANES)], mm.at[n, held], m_s.at[n], m_r.at[n], sib)
             for n in range(D // LANES)]
    for cp in my_m + his_m:
        cp.start()

    half = SIDE // 2

    def first(q):
        up_half = remote(stage.at[q, a2, pl.ds(0, half)], r1.at[q, 0],
                         s1_s.at[q, 0], s1_r.at[q, 0], an)
        down_half = remote(stage.at[q, a2, pl.ds(half, half)], r1.at[q, 1],
                           s1_s.at[q, 1], s1_r.at[q, 1], ap)
        return up_half, down_half

    def alone(q):
        to_next = remote(stage.at[q, a1, pl.ds(half, half)], r2.at[q, 0, pl.ds(half, half)],
                         h_s.at[q, 0], h_r.at[q, 0], an)
        to_prev = remote(stage.at[q, a3, pl.ds(0, half)], r2.at[q, 1, pl.ds(0, half)],
                         h_s.at[q, 1], h_r.at[q, 1], ap)
        return to_next, to_prev

    def second(q):
        to_next = remote(stage.at[q, a1, pl.ds(0, half)], r2.at[q, 0, pl.ds(0, half)],
                         s2_s.at[q, 0], s2_r.at[q, 0], an)
        to_prev = remote(stage.at[q, a3, pl.ds(half, half)], r2.at[q, 1, pl.ds(half, half)],
                         s2_s.at[q, 1], s2_r.at[q, 1], ap)
        return to_next, to_prev

    def third(q):
        return [remote(p2.at[q, t], r3.at[q, i], p_s.at[q, i], p_r.at[q, i], dev)
                for i, (t, dev) in enumerate(((b1, bn), (b3, bp), (b2, bo)))]

    def do_die(q):
        if q + 2 < ROUNDS:
            die(q + 2).start()
            load(q + 2).start()
        load(q).wait()
        die(q).wait_recv()

        def one(e, _):
            for k in range(CHIPS):
                ky, kx = k // SIDE, k % SIDE
                ka = jnp.where(c == 0, kx, ky)
                kb = jnp.where(c == 0, ky, kx)
                rows = pl.ds(ROWS * k, SLOT)
                stage[q, ka, kb, e] = own[q, e, rows, :] + got[q, e, rows, :]
            return 0

        lax.fori_loop(0, MINE, one, 0)
        for cp in first(q) + alone(q):
            cp.start()

    def do_mid(q):
        for side, (tgt, lo) in enumerate(((a1, 0), (a3, half))):
            first(q)[side].wait_recv()

            def one(e, _):
                for k in range(half):
                    stage[q, tgt, lo + k, e] = stage[q, tgt, lo + k, e] + r1[q, side, k, e]
                return 0

            lax.fori_loop(0, MINE, one, 0)
            second(q)[side].start()

    def do_sum(q):
        for cp in alone(q) + second(q):
            cp.wait_recv()

        def one(e, _):
            for k in range(SIDE):
                total = stage[q, a, k, e].astype(jnp.float32) + r2[q, 0, k, e].astype(jnp.float32)
                p2[q, k, e] = (total + r2[q, 1, k, e].astype(jnp.float32)).astype(jnp.bfloat16)
            return 0

        lax.fori_loop(0, MINE, one, 0)
        for cp in third(q):
            cp.start()

    def owner(e):
        oy = e // 2
        ox = oy % 2 + 2 * (e % 2)
        return ((oy * SIDE + ox) * 2 + e // MINE)

    chip = me // 2

    def gather(q, j):
        return remote(bl.at[q, j], xa.at[pl.ds(SLOT * chip, SLOT), cols(q)], g_s.at[q, j],
                      g_r.at[q], (owner(MINE * c + j), z))

    def gather_own(q, j):
        return pltpu.make_async_copy(
            bl.at[q, j], xa.at[pl.ds(SLOT * chip, SLOT), cols(q)], g_r.at[q])

    real = lax.broadcasted_iota(jnp.int32, (SLOT, W), 0) < ROWS

    def do_blend(q):
        for cp in third(q):
            cp.wait_recv()
        if q == 0:
            for cp in my_m + his_m:
                cp.wait()

        def one(j, _):
            total = p2[q, b, j].astype(jnp.float32)
            for i in range(3):
                total = total + r3[q, i, j].astype(jnp.float32)
            before = jnp.concatenate(
                [mm[n, pl.ds(MINE * c + j, SLOT, stride=EXPERTS), :]
                 for n in range(q * W // LANES, (q + 1) * W // LANES)], axis=1)
            after = BETA * before + total
            mo[j, :, cols(q)] = after
            bl[q, j] = jnp.where(real, total + BETA * after, 0.0).astype(jnp.bfloat16)
            there = owner(MINE * c + j)

            @pl.when(there != me)
            def _():
                gather(q, j).start()

            @pl.when(there == me)
            def _():
                gather_own(q, j).start()

            return 0

        lax.fori_loop(0, MINE, one, 0)

    for t in range(ROUNDS + 3):
        if t < ROUNDS:
            do_die(t)
        if 0 <= t - 1 < ROUNDS:
            do_mid(t - 1)
        if 0 <= t - 2 < ROUNDS:
            do_sum(t - 2)
        if 0 <= t - 3 < ROUNDS:
            do_blend(t - 3)

    def window(core):
        return pl.ds(pl.multiple_of(16 * core, 16), 32)

    my_mo = pltpu.make_async_copy(
        mo.at[:, window(c), :], mo_out.at[pl.ds(MINE * c, MINE)], mo_l)
    his_mo = remote(
        mo.at[:, window(1 - c), :], mo_out.at[pl.ds(MINE * c, MINE)], mo_s, mo_r, sib)
    my_mo.start()
    his_mo.start()

    mine = 2 * y + x // 2

    def give(dev):
        k, core = dev // 2, dev % 2
        rows = pl.ds(pl.multiple_of(SLOT * k + 16 * core, 16), 32)
        return remote(up.at[rows, :], up_out.at[mine], u_s.at[dev], u_r, (dev, z))

    def give_own():
        rows = pl.ds(pl.multiple_of(SLOT * chip + 16 * c, 16), 32)
        return pltpu.make_async_copy(up.at[rows, :], up_out.at[mine], u_r)

    @pl.when((x % 2 == y % 2) & (c == y // 2))
    def _():
        for q in range(ROUNDS):
            pltpu.make_async_copy(xa.at[:, cols(q)], xa.at[:, cols(q)], g_r.at[q]).wait()
        steps = TALL // STEP

        def span(i):
            return pl.ds(pl.multiple_of(i * STEP, STEP), STEP)

        def squares(i, acc):
            v = xa[span(i), :].astype(jnp.float32)
            return acc + jnp.sum(v * v, axis=0, keepdims=True)

        total = jnp.sum(lax.fori_loop(0, steps, squares, jnp.zeros((1, D), jnp.float32)),
                        axis=1, keepdims=True)
        scale = 1.0 / (jnp.sqrt(total) + EPS)

        def normalise(i, _):
            xa[span(i), :] = (xa[span(i), :].astype(jnp.float32) * scale).astype(jnp.bfloat16)
            return 0

        lax.fori_loop(0, steps, normalise, 0)

        src, dst = xa, xb
        for turn in range(ITERS):
            last = turn == ITERS - 1

            def gram(i, _, src=src):
                gb[span(i), :] = lax.dot_general(
                    src[span(i), :], src[...], (((1,), (1,)), ((), ())),
                    preferred_element_type=jnp.float32).astype(jnp.bfloat16)
                return 0

            lax.fori_loop(0, steps, gram, 0)

            def apply(i, _, src=src, dst=dst, last=last):
                g = gb[span(i), :]
                squared = jnp.dot(g, gb[...], preferred_element_type=jnp.float32)
                poly = (B * g.astype(jnp.float32) + C * squared).astype(jnp.bfloat16)
                mixed = jnp.dot(poly, src[...], preferred_element_type=jnp.float32)
                new = (A * src[span(i), :].astype(jnp.float32) + mixed)
                if not last:
                    dst[span(i), :] = new.astype(jnp.bfloat16)
                    return 0
                up[span(i), :] = (new.astype(jnp.bfloat16) * 32.0).astype(jnp.bfloat16)

                def send(n, _):
                    dev = i * 2 * (STEP // SLOT) + n

                    @pl.when(dev != me)
                    def _():
                        give(dev).start()

                    @pl.when(dev == me)
                    def _():
                        give_own().start()

                    return 0

                lax.fori_loop(0, 2 * (STEP // SLOT), send, 0)
                return 0

            lax.fori_loop(0, steps, apply, 0)
            src, dst = dst, src

        def sent(dev, _):
            @pl.when(dev != me)
            def _():
                give(dev).wait_send()
            return 0

        lax.fori_loop(0, 2 * CHIPS, sent, 0)

    for q in range(ROUNDS):
        die(q).wait_send()
        for cp in first(q) + alone(q) + second(q):
            cp.wait_send()
        for cp in third(q):
            cp.wait_send()

        def sent(j, _, q=q):
            @pl.when(owner(MINE * c + j) != me)
            def _():
                gather(q, j).wait_send()
            return 0

        lax.fori_loop(0, MINE, sent, 0)
    my_mo.wait()
    his_mo.wait()
    pltpu.make_async_copy(up_out, up_out, u_r).wait()


def reduce_and_step(grads, mom):
    bf, f32 = jnp.bfloat16, jnp.float32
    dma = pltpu.SemaphoreType.DMA
    half = SIDE // 2
    return pl.pallas_call(
        kernel,
        out_shape=(
            jax.ShapeDtypeStruct((EXPERTS, 32, D), f32),
            jax.ShapeDtypeStruct((EXPERTS, 32, D), bf),
        ),
        in_specs=[pl.BlockSpec(memory_space=pl.ANY)] * 2,
        out_specs=(pl.BlockSpec(memory_space=pl.ANY),) * 2,
        scratch_shapes=[
            pltpu.VMEM((ROUNDS, MINE, HELD, W), bf),
            pltpu.VMEM((ROUNDS, MINE, HELD, W), bf),
            pltpu.VMEM((ROUNDS, SIDE, SIDE, MINE, SLOT, W), bf),
            pltpu.VMEM((ROUNDS, 2, half, MINE, SLOT, W), bf),
            pltpu.VMEM((ROUNDS, 2, SIDE, MINE, SLOT, W), bf),
            pltpu.VMEM((ROUNDS, SIDE, MINE, SLOT, W), bf),
            pltpu.VMEM((ROUNDS, 3, MINE, SLOT, W), bf),
            pltpu.VMEM((ROUNDS, MINE, SLOT, W), bf),
            pltpu.VMEM((D // LANES, SLOT * EXPERTS, LANES), f32),
            pltpu.VMEM((MINE, SLOT, D), f32),
            pltpu.VMEM((TALL, D), bf),
            pltpu.VMEM((TALL, D), bf),
            pltpu.VMEM((TALL, TALL), bf),
            pltpu.VMEM((TALL, D), bf),
            dma((ROUNDS,)), dma((ROUNDS,)), dma((ROUNDS,)),
            dma((ROUNDS, 2)), dma((ROUNDS, 2)),
            dma((ROUNDS, 2)), dma((ROUNDS, 2)),
            dma((ROUNDS, 2)), dma((ROUNDS, 2)),
            dma((ROUNDS, 3)), dma((ROUNDS, 3)),
            dma((ROUNDS, MINE)), dma((ROUNDS,)),
            dma((D // LANES,)), dma((D // LANES,)), dma((D // LANES,)),
            dma(()), dma(()), dma(()),
            dma((2 * CHIPS,)), dma(()),
        ],
        compiler_params=pltpu.CompilerParams(
            collective_id=0, has_side_effects=True, vmem_limit_bytes=60 * 2**20),
        name="muon",
    )(grads, mom)


def per_device(grads, momentum):
    c = lax.axis_index("dp") % 2
    mom = jnp.transpose(momentum, (1, 0, 2)).reshape(OWN * EXPERTS, D)
    mo, up = reduce_and_step(grads[0], mom)
    skip = (OWN - 16) * c
    return (lax.dynamic_slice_in_dim(mo, skip, OWN, 1), lax.dynamic_slice_in_dim(up, skip, OWN, 1))


def solution(mesh):
    return jax.shard_map(
        per_device,
        mesh=mesh,
        in_specs=(P("dp", "expert", None, None), P("expert", "dp", None)),
        out_specs=(P("expert", "dp", None), P("expert", "dp", None)),
        check_vma=False,
    )
```

time: 285 us -> 92.9 us (0.33)
  waiting for transfers between devices: 201 us -> 0 us
  Pallas kernels: 0 us -> 86 us
  starting transfers between devices: 42.9 us -> 0 us
  local copies, waits for them, and re-layouts: 24.3 us -> 4.71 us
  between operations: 14.1 us -> 0.67 us
    reduce_scatter x1 -> x0, waiting for transfers between devices: 111 us -> none  [per_device(): lax.psum_scatter(local_grads.astype(jnp.float32).astype(jnp.bfloat16), 'd...]
    pallas_call x0 -> x1, Pallas kernels: none -> 86 us  [reduce_and_step(): pl.pallas_call(kernel, out_shape=(jax.ShapeDtypeStruct((EXPERTS, 32, D),...]
    all_gather x1 -> x0, waiting for transfers between devices: 66.1 us -> none  [per_device(): gathered = lax.all_gather(blended, 'dp', axis=1, tiled=True)]
    all_to_all x1 -> x0, starting transfers between devices: 42.8 us -> none  [per_device(): lax.all_to_all(sending, 'dp', split_axis=0, concat_axis=0, tiled=True)]
    all_to_all x1 -> x0, waiting for transfers between devices: 23.9 us -> none  [per_device(): lax.all_to_all(sending, 'dp', split_axis=0, concat_axis=0, tiled=True)]
    unnamed x4 -> x2, local copies, waits for them, and re-layouts: 22.2 us -> 2.22 us
  transfers between devices with their start and end apart: 3 -> 0, of which waited for: 3 -> 0; matrix products, arithmetic and copies ran while one was open for 0% -> 0% of each run, Pallas kernels for 0% -> 0%
where the time goes in v1:
time: 92.9 us; the launch traced here: 91.4 us
  Pallas kernels  86 us (93%)
  local copies, waits for them, and re-layouts  4.71 us (5%)
    pallas_call x1, Pallas kernels, reduce_and_step(): pl.pallas_call(kernel, out_shape=(jax.ShapeDtypeStruct((EXPERTS, 32, D),...  86 us
    unnamed x2, local copies, waits for them, and re-layouts  2.22 us

profile of v1, /device:TPU:64, one launch (start us, length us, event | category | flops | bytes accessed | tf_op | source)
XLA Modules:
  0.0 91.4 jit_solution(4861512176082578448)
XLA Ops:
  0.6 86.0 %muon.1 = (f32[8,32,1024]{2,1,0:T(8,128)}, bf16[8,32,1024]{2,1,0:T(8,128)(2,1)}) custom-call(bf16[8,704,1024]{2,1,0:T(8,128)(2,1)} %bitcast.4, f32[176,1024]{1,0:T(8,128)} %bitcast.5), custom_call_target="tpu_custom_call" | custom-call | tf_op jit(solution)/shard_map/muon/pallas_call | solution.py:337
  86.6 1.3 %constant_dynamic-slice_fusion.1 = f32[8,22,1024]{2,1,0:T(8,128)S(1)} fusion(f32[8,32,1024]{2,1,0:T(8,128)} %get-tuple-element.4, s32[]{:T(128)S(6)} %select_n.12), kind=kLoop, calls=%fused_computation.1 | loop fusion | bytes 1441796 | tf_op jit(solution)/shard_map/dynamic_slice | solution.py:381
  88.0 1.2 %constant_dynamic-slice_fusion = bf16[8,22,1024]{2,1,0:T(8,128)(2,1)S(1)} fusion(bf16[8,32,1024]{2,1,0:T(8,128)(2,1)} %get-tuple-element.5, s32[]{:T(128)S(6)} %select_n.12), kind=kLoop, calls=%fused_computation | loop fusion | bytes 720900 | tf_op jit(solution)/shard_map/dynamic_slice | solution.py:381
  89.2 1.3 %copy.4 = f32[8,22,1024]{2,0,1:T(8,128)} copy(f32[8,22,1024]{2,1,0:T(8,128)S(1)} %constant_dynamic-slice_fusion.1) | data formatting | bytes 1441792
  90.4 0.9 %copy.5 = bf16[8,22,1024]{2,0,1:T(8,128)(2,1)} copy(bf16[8,22,1024]{2,1,0:T(8,128)(2,1)S(1)} %constant_dynamic-slice_fusion) | data formatting | bytes 720896

commit v2 on v1

v2 whole, which is shorter than its diff:
```python
import functools

import jax
import jax.numpy as jnp
from jax import lax
from jax.experimental import pallas as pl
from jax.experimental.pallas import tpu as pltpu
from jax.sharding import PartitionSpec as P

MESH = pl.DeviceIdType.MESH
ITERS = 3
A, B, C = 3.4445, -4.775, 2.0315
BETA = 0.95
EPS = 1e-07

SIDE = 4
CHIPS = SIDE * SIDE
EXPERTS = 8
MINE = 4
HID, D = 704, 1024
ROWS = HID // CHIPS
SLOT = 48
QUARTER = HID // SIDE
OWN = HID // (2 * CHIPS)
ROUNDS = 8
DIRECT = 3
RELAYED = 5
W = D // ROUNDS
TALL = CHIPS * SLOT
LANES = 128
LEFT = 512
PARTS = 2
PART = LEFT // PARTS
BLOCK = 256
STRIP = 128


def kernel(grads, mom, mo_out, up_out, own, got, stage, r1a, r2a, p2, r1b, r2b, r3, bl, mm, ms,
           xa, xb, gb, pb, up, rb, lb, own_s, die_ss, die_rs, s1_s, s1_r, s2_s, s2_r, h_s, h_r,
           p_s, p_r, g_s, g_r, b_s, b_r, m_l, m_s, m_r, mo_l, mo_s, mo_r, l_s, l_r, v_s, u_s, u_r):
    me = lax.axis_index("dp")
    z = lax.axis_index("expert")
    c = me % 2
    x = (me // 2) % SIDE
    y = me // (2 * SIDE)
    a = jnp.where(c == 0, x, y)
    b = jnp.where(c == 0, y, x)

    def at(a_, b_):
        a_, b_ = a_ % SIDE, b_ % SIDE
        row = jnp.where(c == 0, b_, a_)
        col = jnp.where(c == 0, a_, b_)
        return ((row * SIDE + col) * 2 + c, z)

    sib = (me + 1 - 2 * c, z)
    an, ap = at(a + 1, b), at(a + 3, b)
    bn, bp, bo = at(a, b + 1), at(a, b + 3), at(a, b + 2)
    a1, a2, a3 = (a + 1) % SIDE, (a + 2) % SIDE, (a + 3) % SIDE
    b1, b2, b3 = (b + 1) % SIDE, (b + 2) % SIDE, (b + 3) % SIDE

    def remote(src, dst, ss, rs, dev):
        return pltpu.make_async_remote_copy(
            src, dst, ss, rs, device_id=dev, device_id_type=MESH)

    def cols(q):
        return pl.ds(q * W, W)

    def load(q):
        return pltpu.make_async_copy(
            grads.at[pl.ds(MINE * c, MINE), :, cols(q)], own.at[q], own_s.at[q])

    load(0).start()
    load(1).start()

    barrier = pltpu.get_barrier_semaphore()
    for dev in (sib, an, ap, bn, bp, bo):
        pl.semaphore_signal(barrier, inc=1, device_id=dev, device_id_type=MESH)
    pl.semaphore_wait(barrier, 6)

    def die(q):
        return remote(grads.at[pl.ds(MINE * (1 - c), MINE), :, cols(q)], got.at[q],
                      die_ss.at[q], die_rs.at[q], sib)

    die(0).start()
    die(1).start()
    held = pl.ds(pl.multiple_of(OWN * EXPERTS * c, 8), OWN * EXPERTS)
    my_m = [pltpu.make_async_copy(
        mom.at[:, pl.ds(LANES * n, LANES)], mm.at[n, held], m_l.at[n]) for n in range(D // LANES)]
    his_m = [remote(mom.at[:, pl.ds(LANES * n, LANES)], mm.at[n, held], m_s.at[n], m_r.at[n], sib)
             for n in range(D // LANES)]
    for cp in my_m + his_m:
        cp.start()

    half = MINE // 2
    lower, upper = pl.ds(0, half), pl.ds(half, half)

    ringed = ROUNDS - DIRECT
    phases = ((stage, r1a, r2a, (a1, a2, a3), an, ap), (p2, r1b, r2b, (b1, b2, b3), bn, bp))

    def first(f, q):
        src, r1, _, (_, far, _), following, previous = phases[f]
        return (remote(src.at[q, far, lower], r1.at[q, 0], s1_s.at[f, q, 0], s1_r.at[f, q, 0],
                       following),
                remote(src.at[q, far, upper], r1.at[q, 1], s1_s.at[f, q, 1], s1_r.at[f, q, 1],
                       previous))

    def alone(f, q):
        src, _, r2, (near, _, back), following, previous = phases[f]
        return (remote(src.at[q, near, upper], r2.at[q, 0, upper], h_s.at[f, q, 0],
                       h_r.at[f, q, 0], following),
                remote(src.at[q, back, lower], r2.at[q, 1, lower], h_s.at[f, q, 1],
                       h_r.at[f, q, 1], previous))

    def second(f, q):
        src, _, r2, (near, _, back), following, previous = phases[f]
        return (remote(src.at[q, near, lower], r2.at[q, 0, lower], s2_s.at[f, q, 0],
                       s2_r.at[f, q, 0], following),
                remote(src.at[q, back, upper], r2.at[q, 1, upper], s2_s.at[f, q, 1],
                       s2_r.at[f, q, 1], previous))

    def third(q):
        d = q - ringed
        return [remote(p2.at[q, t], r3.at[d, i], p_s.at[d, i], p_r.at[d, i], dev)
                for i, (t, dev) in enumerate(((b1, bn), (b3, bp), (b2, bo)))]

    def do_die(q):
        if q + 2 < ROUNDS:
            die(q + 2).start()
            load(q + 2).start()
        load(q).wait()
        die(q).wait_recv()

        @pl.when(c == 1)
        def _():
            def one(e, _):
                for k in range(SIDE):
                    rows = pl.ds(QUARTER * k, QUARTER)
                    stage[q, k, e] = own[q, e, rows, :] + got[q, e, rows, :]
                return 0

            lax.fori_loop(0, MINE, one, 0)

        @pl.when(c == 0)
        def _():
            def one(e, _):
                for k in range(CHIPS):
                    rows = pl.ds(ROWS * k, ROWS)
                    stage[q, k % SIDE, e, pl.ds(ROWS * (k // SIDE), ROWS), :] = (
                        own[q, e, rows, :] + got[q, e, rows, :])
                return 0

            lax.fori_loop(0, MINE, one, 0)

        for cp in first(0, q) + alone(0, q):
            cp.start()

    def do_mid(f, q):
        src, r1, _, (near, _, back), _, _ = phases[f]
        for side, (tgt, lo) in enumerate(((near, 0), (back, half))):
            first(f, q)[side].wait_recv()

            def one(e, _):
                src[q, tgt, lo + e] = src[q, tgt, lo + e] + r1[q, side, e]
                return 0

            lax.fori_loop(0, half, one, 0)
            second(f, q)[side].start()

    def do_sum(q):
        for cp in alone(0, q) + second(0, q):
            cp.wait_recv()

        def one(e, _):
            total = stage[q, a, e].astype(jnp.float32) + r2a[q, 0, e].astype(jnp.float32)
            total = total + r2a[q, 1, e].astype(jnp.float32)
            for k in range(SIDE):
                p2[q, k, e, pl.ds(0, ROWS), :] = (
                    total[ROWS * k:ROWS * (k + 1)].astype(jnp.bfloat16))
            return 0

        lax.fori_loop(0, MINE, one, 0)
        for cp in third(q) if q >= ringed else first(1, q) + alone(1, q):
            cp.start()

    def owner(e):
        oy = e // 2
        ox = oy % 2 + 2 * (e % 2)
        return oy, ox, (oy * SIDE + ox) * 2 + e // MINE

    chip = me // 2
    here = pl.ds(pl.multiple_of(SLOT * chip, 16), SLOT)

    def gather(q, j, dev):
        return remote(bl.at[q, j], xa.at[here, cols(q)], g_s.at[q, j], g_r.at[q], (dev, z))

    def gather_own(q, j):
        return pltpu.make_async_copy(bl.at[q, j], xa.at[here, cols(q)], g_r.at[q])

    def gather_row(q, j, oy):
        row = (y - oy) % SIDE - 1
        return remote(bl.at[q, j], rb.at[q, row], g_s.at[q, j], b_r.at[q, row],
                      ((oy * SIDE + x) * 2 + c, z))

    def relay(q, row):
        there = pl.ds(pl.multiple_of(SLOT * (((y + row + 1) % SIDE) * SIDE + x), 16), SLOT)
        dev = (y * SIDE + y % 2 + 2 * (q % 2)) * 2 + c
        return remote(rb.at[q, row], xa.at[there, cols(q)], b_s.at[q, row], g_r.at[q], (dev, z))

    def relays(q):
        return (c == y // 2) & (x != y % 2 + 2 * (q % 2))

    def do_relay(q):
        @pl.when(relays(q))
        def _():
            for row in range(SIDE - 1):
                landed = rb.at[q, row]
                pltpu.make_async_copy(landed, landed, b_r.at[q, row]).wait()
                relay(q, row).start()

    real = lax.broadcasted_iota(jnp.int32, (SLOT, W), 0) < ROWS

    def do_blend(q):
        for cp in third(q) if q >= ringed else alone(1, q) + second(1, q):
            cp.wait_recv()
        came = ([r3.at[q - ringed, i] for i in range(3)] if q >= ringed
                else [r2b.at[q, i] for i in range(2)])
        if q == 0:
            for cp in my_m + his_m:
                cp.wait()

        def one(j, _):
            total = p2[q, b, j].astype(jnp.float32)
            for ref in came:
                total = total + ref[j].astype(jnp.float32)
            turns = range(q * W // LANES, (q + 1) * W // LANES)
            these = pl.ds(MINE * c + j, SLOT, stride=EXPERTS)
            before = jnp.concatenate([mm[n, these, :] for n in turns], axis=1)
            after = BETA * before + total
            for i, n in enumerate(turns):
                mm[n, these, :] = after[:, i * LANES:(i + 1) * LANES]
            bl[q, j] = jnp.where(real, total + BETA * after, 0.0).astype(jnp.bfloat16)
            oy, ox, there = owner(MINE * c + j)
            turned = (x != ox) & (y != oy) & (j % 2 == q % 2) if q < RELAYED else False

            @pl.when(there == me)
            def _():
                gather_own(q, j).start()

            @pl.when((there != me) & jnp.logical_not(turned))
            def _():
                gather(q, j, there).start()

            if q < RELAYED:
                @pl.when(turned)
                def _():
                    gather_row(q, j, oy).start()

            return 0

        lax.fori_loop(0, MINE, one, 0)

    for t in range(ROUNDS + 4):
        if t < ROUNDS:
            do_die(t)
        if 0 <= t - 1 < ROUNDS:
            do_mid(0, t - 1)
        if 0 <= t - 2 < ROUNDS:
            do_sum(t - 2)
        if 0 <= t - 3 < ringed:
            do_mid(1, t - 3)
        if 0 <= t - 4 < ringed:
            do_blend(t - 4)
        if 0 <= t - 5 < RELAYED:
            do_relay(t - 5)
        if ringed <= t - 3 < ROUNDS:
            do_blend(t - 3)

    def share(core):
        return pl.ds(pl.multiple_of(OWN * EXPERTS * core, 8), OWN * EXPERTS)

    my_mo = [pltpu.make_async_copy(
        mm.at[n, share(c)], mo_out.at[:, pl.ds(LANES * n, LANES)], mo_l.at[n])
        for n in range(D // LANES)]
    his_mo = [remote(mm.at[n, share(1 - c)], ms.at[n], mo_s.at[n], mo_r.at[n], sib)
              for n in range(D // LANES)]
    for cp in his_mo:
        cp.start()

    def finish_mo():
        row = lax.broadcasted_iota(jnp.int32, (OWN * EXPERTS, LANES), 0)
        ours = (row % EXPERTS) // MINE == c
        for n in range(D // LANES):
            his_mo[n].wait_recv()
            mm[n, share(c), :] = jnp.where(ours, mm[n, share(c), :], ms[n])
            my_mo[n].start()

    oy = x % 2 + 2 * c
    mine = 2 * oy + x // 2
    right = pl.ds(LEFT, D - LEFT)

    def left(part):
        return pl.ds(PART * part, PART)

    def give_row(part, d):
        row = (oy + d) % SIDE
        rows = pl.ds(pl.multiple_of(SIDE * SLOT * row, 16), SIDE * SLOT)
        return remote(up.at[rows, left(part)], lb.at[part], l_s.at[part, d - 1], l_r.at[part],
                      ((row * SIDE + x) * 2 + c, z))

    def give(dev):
        rows = pl.ds(pl.multiple_of(SLOT * (dev // 2) + 16 * (dev % 2), 16), 32)
        return remote(up.at[rows, right], up_out.at[mine, :, right], u_s.at[dev], u_r, (dev, z))

    def give_own():
        rows = pl.ds(pl.multiple_of(SLOT * chip + 16 * c, 16), 32)
        return pltpu.make_async_copy(up.at[rows, right], up_out.at[mine, :, right], u_r)

    def spread(src, base, part, n):
        dev = (y * SIDE) * 2 + n
        rows = pl.ds(pl.multiple_of(base + SLOT * (n // 2) + 16 * (n % 2), 16), 32)
        return remote(src.at[rows], up_out.at[mine, :, left(part)], v_s.at[part, n], u_r, (dev, z))

    def spread_all(src, base, part):
        def one(n, _):
            @pl.when(y * SIDE * 2 + n != me)
            def _():
                spread(src, base, part, n).start()
            return 0

        lax.fori_loop(0, 2 * SIDE, one, 0)
        rows = pl.ds(pl.multiple_of(base + SLOT * x + 16 * c, 16), 32)
        pltpu.make_async_copy(src.at[rows], up_out.at[mine, :, left(part)], u_r).start()

    @pl.when(y == oy)
    def _():
        for q in range(ROUNDS):
            pltpu.make_async_copy(xa.at[:, cols(q)], xa.at[:, cols(q)], g_r.at[q]).wait()
        blocks = [slice(i * BLOCK, (i + 1) * BLOCK) for i in range(TALL // BLOCK)]
        strips = [slice(i * STRIP, (i + 1) * STRIP) for i in range(TALL // STRIP)]
        total = jnp.zeros((1, D), jnp.float32)
        for rows in strips:
            v = xa[rows, :].astype(jnp.float32)
            total = total + jnp.sum(v * v, axis=0, keepdims=True)
        scale = 1.0 / (jnp.sqrt(jnp.sum(total, axis=1, keepdims=True)) + EPS)
        for rows in strips:
            xa[rows, :] = (xa[rows, :].astype(jnp.float32) * scale).astype(jnp.bfloat16)

        src, dst = xa, xb
        for turn in range(ITERS):
            for i, rows in enumerate(blocks):
                for j in range(i, len(blocks)):
                    block = lax.dot_general(
                        src[rows, :], src[blocks[j], :], (((1,), (1,)), ((), ())),
                        preferred_element_type=jnp.float32)
                    gb[rows, blocks[j]] = block.astype(jnp.bfloat16)
                    if j > i:
                        gb[blocks[j], rows] = block.T.astype(jnp.bfloat16)
            for i, rows in enumerate(blocks):
                for j in range(i, len(blocks)):
                    squared = jnp.dot(gb[rows, :], gb[:, blocks[j]],
                                      preferred_element_type=jnp.float32)
                    poly = (B * gb[rows, blocks[j]].astype(jnp.float32)
                            + C * squared).astype(jnp.bfloat16)
                    pb[rows, blocks[j]] = poly
                    if j > i:
                        pb[blocks[j], rows] = poly.T
            if turn < ITERS - 1:
                for rows in strips:
                    mixed = jnp.dot(pb[rows, :], src[...], preferred_element_type=jnp.float32)
                    dst[rows, :] = (A * src[rows, :].astype(jnp.float32) + mixed).astype(
                        jnp.bfloat16)
                src, dst = dst, src
                continue
            for part in range(PARTS + 1):
                these = slice(PART * part, PART * (part + 1) if part < PARTS else D)
                for rows in strips:
                    mixed = jnp.dot(pb[rows, :], src[:, these], preferred_element_type=jnp.float32)
                    new = (A * src[rows, these].astype(jnp.float32) + mixed).astype(jnp.bfloat16)
                    up[rows, these] = (new.astype(jnp.float32) * 32.0).astype(jnp.bfloat16)
                if part < PARTS:
                    for d in (2, 1, 3):
                        give_row(part, d).start()
                    spread_all(up.at[:, left(part)], SIDE * SLOT * y, part)

        def send(dev, _):
            @pl.when(dev != me)
            def _():
                give(dev).start()
            return 0

        lax.fori_loop(0, 2 * CHIPS, send, 0)
        give_own().start()
        finish_mo()

        def sent(dev, _):
            @pl.when(dev != me)
            def _():
                give(dev).wait_send()
            return 0

        lax.fori_loop(0, 2 * CHIPS, sent, 0)
        for part in range(PARTS):
            for d in range(1, SIDE):
                give_row(part, d).wait_send()

    @pl.when(y != oy)
    def _():
        finish_mo()
        for part in range(PARTS):
            give_row(part, 1).wait_recv()
            spread_all(lb.at[part], 0, part)

    for q in range(ROUNDS):
        die(q).wait_send()
        for f in range(2):
            if f == 0 or q < ringed:
                for cp in first(f, q) + alone(f, q) + second(f, q):
                    cp.wait_send()
        if q >= ringed:
            for cp in third(q):
                cp.wait_send()

        def sent(j, _, q=q):
            @pl.when(owner(MINE * c + j)[2] != me)
            def _():
                gather(q, j, sib[0]).wait_send()
            return 0

        lax.fori_loop(0, MINE, sent, 0)
        if q < RELAYED:
            @pl.when(relays(q))
            def _(q=q):
                for row in range(SIDE - 1):
                    relay(q, row).wait_send()
    for n in range(D // LANES):
        his_mo[n].wait_send()
        my_mo[n].wait()

    for part in range(PARTS):
        def spread_sent(n, _, part=part):
            @pl.when(y * SIDE * 2 + n != me)
            def _():
                spread(lb.at[part], 0, part, n).wait_send()
            return 0

        lax.fori_loop(0, 2 * SIDE, spread_sent, 0)
    pltpu.make_async_copy(up_out, up_out, u_r).wait()


def reduce_and_step(grads, mom):
    bf, f32 = jnp.bfloat16, jnp.float32
    dma = pltpu.SemaphoreType.DMA
    half = MINE // 2
    tiles = D // LANES
    return pl.pallas_call(
        kernel,
        out_shape=(
            jax.ShapeDtypeStruct((OWN * EXPERTS, D), f32),
            jax.ShapeDtypeStruct((EXPERTS, 32, D), bf),
        ),
        in_specs=[pl.BlockSpec(memory_space=pl.ANY)] * 2,
        out_specs=(pl.BlockSpec(memory_space=pl.ANY),) * 2,
        scratch_shapes=[
            pltpu.VMEM((ROUNDS, MINE, HID, W), bf),
            pltpu.VMEM((ROUNDS, MINE, HID, W), bf),
            pltpu.VMEM((ROUNDS, SIDE, MINE, QUARTER, W), bf),
            pltpu.VMEM((ROUNDS, 2, half, QUARTER, W), bf),
            pltpu.VMEM((ROUNDS, 2, MINE, QUARTER, W), bf),
            pltpu.VMEM((ROUNDS, SIDE, MINE, SLOT, W), bf),
            pltpu.VMEM((ROUNDS, 2, half, SLOT, W), bf),
            pltpu.VMEM((ROUNDS, 2, MINE, SLOT, W), bf),
            pltpu.VMEM((DIRECT, 3, MINE, SLOT, W), bf),
            pltpu.VMEM((ROUNDS, MINE, SLOT, W), bf),
            pltpu.VMEM((tiles, SLOT * EXPERTS, LANES), f32),
            pltpu.VMEM((tiles, OWN * EXPERTS, LANES), f32),
            pltpu.VMEM((TALL, D), bf),
            pltpu.VMEM((TALL, D), bf),
            pltpu.VMEM((TALL, TALL), bf),
            pltpu.VMEM((TALL, TALL), bf),
            pltpu.VMEM((TALL, D), bf),
            pltpu.VMEM((RELAYED, SIDE - 1, SLOT, W), bf),
            pltpu.VMEM((PARTS, SIDE * SLOT, PART), bf),
            dma((ROUNDS,)), dma((ROUNDS,)), dma((ROUNDS,)),
            dma((2, ROUNDS, 2)), dma((2, ROUNDS, 2)),
            dma((2, ROUNDS, 2)), dma((2, ROUNDS, 2)),
            dma((2, ROUNDS, 2)), dma((2, ROUNDS, 2)),
            dma((DIRECT, 3)), dma((DIRECT, 3)),
            dma((ROUNDS, MINE)), dma((ROUNDS,)),
            dma((RELAYED, SIDE - 1)), dma((RELAYED, SIDE - 1)),
            dma((tiles,)), dma((tiles,)), dma((tiles,)),
            dma((tiles,)), dma((tiles,)), dma((tiles,)),
            dma((PARTS, SIDE - 1)), dma((PARTS,)),
            dma((PARTS, 2 * SIDE)),
            dma((2 * CHIPS,)), dma(()),
        ],
        compiler_params=pltpu.CompilerParams(
            collective_id=0, has_side_effects=True, vmem_limit_bytes=48 * 2**20),
        name="muon",
    )(grads, mom)


def per_device(grads, momentum):
    c = lax.axis_index("dp") % 2
    mom = jnp.transpose(momentum, (1, 0, 2)).reshape(OWN * EXPERTS, D)
    mo, up = reduce_and_step(grads[0], mom)
    mo = jnp.transpose(mo.reshape(OWN, EXPERTS, D), (1, 0, 2))
    return mo, lax.dynamic_slice_in_dim(up, (OWN - 16) * c, OWN, 1)


def solution(mesh):
    return jax.shard_map(
        per_device,
        mesh=mesh,
        in_specs=(P("dp", "expert", None, None), P("expert", "dp", None)),
        out_specs=(P("expert", "dp", None), P("expert", "dp", None)),
        check_vma=False,
    )
```

time: 92.9 us -> 78.7 us (0.85)
  Pallas kernels: 86 us -> 74.3 us
  local copies, waits for them, and re-layouts: 4.71 us -> 3.01 us
    pallas_call x1, Pallas kernels: 86 us -> 74.3 us  [reduce_and_step(): pl.pallas_call(kernel, out_shape=(jax.ShapeDtypeStruct((OWN * EXPERTS, D)...]
    dynamic_slice x2 -> x1, local copies, waits for them, and re-layouts: 2.5 us -> 0.11 us  [per_device(): return (mo, lax.dynamic_slice_in_dim(up, (OWN - 16) * c, OWN, 1))]
    unnamed x2 -> x4, local copies, waits for them, and re-layouts: 2.22 us -> 2.9 us
where the time goes in v2:
time: 78.7 us; the launch traced here: 78 us
  Pallas kernels  74.3 us (94%)
  local copies, waits for them, and re-layouts  3.01 us (4%)
    pallas_call x1, Pallas kernels, reduce_and_step(): pl.pallas_call(kernel, out_shape=(jax.ShapeDtypeStruct((OWN * EXPERTS, D)...  74.3 us
    unnamed x4, local copies, waits for them, and re-layouts  2.9 us

profile of v2, /device:TPU:64, one launch (start us, length us, event | category | flops | bytes accessed | tf_op | source)
XLA Modules:
  0.0 78.0 jit_solution(7719197988420430349)
XLA Ops:
  0.6 0.0 copy-start
  0.7 1.1 %copy-done = f32[8,22,1024]{2,0,1:T(8,128)S(1)} copy-done((f32[8,22,1024]{2,0,1:T(8,128)S(1)}, f32[8,22,1024]{2,0,1:T(8,128)}, u32[]{:S(2)}) %copy-start) | copy-done | bytes 720920
  1.8 74.3 %muon.1 = (f32[176,1024]{1,0:T(8,128)S(1)}, bf16[8,32,1024]{2,1,0:T(8,128)(2,1)S(1)}) custom-call(bf16[8,704,1024]{2,1,0:T(8,128)(2,1)} %bitcast.9, f32[176,1024]{1,0:T(8,128)S(1)} %bitcast.8), custom_call_target="tpu_custom_call" | custom-call | tf_op jit(solution)/shard_map/muon/pallas_call | solution.py:455
  76.1 0.1 constant_dynamic-slice_fusion
  76.2 0.9 %copy.4 = bf16[8,22,1024]{2,0,1:T(8,128)(2,1)} copy(bf16[8,22,1024]{2,1,0:T(8,128)(2,1)S(1)} %constant_dynamic-slice_fusion) | data formatting | bytes 720896
  77.1 0.9 %copy.6 = f32[8,22,1024]{2,0,1:T(8,128)} copy(f32[8,22,1024]{2,0,1:T(8,128)S(1)} %bitcast.7) | data formatting | bytes 1441792
Async XLA Ops:
  0.6 1.1 %copy-start = (f32[8,22,1024]{2,0,1:T(8,128)S(1)}, f32[8,22,1024]{2,0,1:T(8,128)}, u32[]{:S(2)}) copy-start(f32[8,22,1024]{2,0,1:T(8,128)} %param.3) | copy-start | bytes 2162692

commit v3 on v2

--- a/solution.py
+++ b/solution.py
@@ -23,8 +23,9 @@
 QUARTER = HID // SIDE
 OWN = HID // (2 * CHIPS)
 ROUNDS = 8
+LAG = 5
 DIRECT = 3
-RELAYED = 5
+RELAYED = 2
 W = D // ROUNDS
 TALL = CHIPS * SLOT
 LANES = 128
@@ -33,10 +34,11 @@
 PART = LEFT // PARTS
 BLOCK = 256
 STRIP = 128
+EARLY = 4
 
 
 def kernel(grads, mom, mo_out, up_out, own, got, stage, r1a, r2a, p2, r1b, r2b, r3, bl, mm, ms,
-           xa, xb, gb, pb, up, rb, lb, own_s, die_ss, die_rs, s1_s, s1_r, s2_s, s2_r, h_s, h_r,
+           xa, xb, ga, gb, pb, up, rb, lb, own_s, die_ss, die_rs, s1_s, s1_r, s2_s, s2_r, h_s, h_r,
            p_s, p_r, g_s, g_r, b_s, b_r, m_l, m_s, m_r, mo_l, mo_s, mo_r, l_s, l_r, v_s, u_s, u_r):
     me = lax.axis_index("dp")
     z = lax.axis_index("expert")
@@ -259,21 +261,18 @@
 
         lax.fori_loop(0, MINE, one, 0)
 
-    for t in range(ROUNDS + 4):
-        if t < ROUNDS:
-            do_die(t)
-        if 0 <= t - 1 < ROUNDS:
-            do_mid(0, t - 1)
-        if 0 <= t - 2 < ROUNDS:
-            do_sum(t - 2)
-        if 0 <= t - 3 < ringed:
-            do_mid(1, t - 3)
-        if 0 <= t - 4 < ringed:
-            do_blend(t - 4)
-        if 0 <= t - 5 < RELAYED:
-            do_relay(t - 5)
-        if ringed <= t - 3 < ROUNDS:
-            do_blend(t - 3)
+    end = ROUNDS + 1
+    steps = []
+    for q in range(ROUNDS):
+        steps += [(q, 0, q, do_die), (q + 1, 1, q, functools.partial(do_mid, 0)),
+                  (min(q + LAG, end), 2, q, do_sum)]
+        if q < ringed:
+            steps.append((min(q + LAG + 1, end), 3, q, functools.partial(do_mid, 1)))
+        steps.append((min(q + LAG + (2 if q < ringed else 1), end), 4, q, do_blend))
+        if q < RELAYED:
+            steps.append((min(q + LAG + 3, end), 5, q, do_relay))
+    for _, _, q, step in sorted(steps, key=lambda item: item[:3]):
+        step(q)
 
     def share(core):
         return pl.ds(pl.multiple_of(OWN * EXPERTS * core, 8), OWN * EXPERTS)
@@ -333,37 +332,58 @@
 
     @pl.when(y == oy)
     def _():
-        for q in range(ROUNDS):
-            pltpu.make_async_copy(xa.at[:, cols(q)], xa.at[:, cols(q)], g_r.at[q]).wait()
         blocks = [slice(i * BLOCK, (i + 1) * BLOCK) for i in range(TALL // BLOCK)]
         strips = [slice(i * STRIP, (i + 1) * STRIP) for i in range(TALL // STRIP)]
-        total = jnp.zeros((1, D), jnp.float32)
-        for rows in strips:
-            v = xa[rows, :].astype(jnp.float32)
-            total = total + jnp.sum(v * v, axis=0, keepdims=True)
-        scale = 1.0 / (jnp.sqrt(jnp.sum(total, axis=1, keepdims=True)) + EPS)
+        pairs = [(rows, others) for i, rows in enumerate(blocks) for others in blocks[i:]]
+
+        def arrived(q):
+            pltpu.make_async_copy(xa.at[:, cols(q)], xa.at[:, cols(q)], g_r.at[q]).wait()
+
+        def products(rows, others, part, matrix):
+            return lax.dot_general(
+                matrix[rows, part], matrix[others, part], (((1,), (1,)), ((), ())),
+                preferred_element_type=jnp.float32)
+
+        def squares(part):
+            total = jnp.zeros((1, part.stop - part.start), jnp.float32)
+            for rows in strips:
+                v = xa[rows, part].astype(jnp.float32)
+                total = total + jnp.sum(v * v, axis=0, keepdims=True)
+            return jnp.sum(total, axis=1, keepdims=True)
+
+        def put(rows, others, block):
+            gb[rows, others] = block.astype(jnp.bfloat16)
+            if others.start > rows.start:
+                gb[others, rows] = block.T.astype(jnp.bfloat16)
+
+        head, tail = slice(0, EARLY * W), slice(EARLY * W, D)
+        for q in range(EARLY):
+            arrived(q)
+        for rows, others in pairs:
+            ga[rows, others] = products(rows, others, head, xa)
+        norm = squares(head)
+        for q in range(EARLY, ROUNDS):
+            arrived(q)
+        norm = jnp.sqrt(norm + squares(tail))
+        scale = 1.0 / (norm + EPS)
+        for rows, others in pairs:
+            block = ga[rows, others] + products(rows, others, tail, xa)
+            put(rows, others, block * (scale * scale))
         for rows in strips:
             xa[rows, :] = (xa[rows, :].astype(jnp.float32) * scale).astype(jnp.bfloat16)
 
         src, dst = xa, xb
         for turn in range(ITERS):
-            for i, rows in enumerate(blocks):
-                for j in range(i, len(blocks)):
-                    block = lax.dot_general(
-                        src[rows, :], src[blocks[j], :], (((1,), (1,)), ((), ())),
-                        preferred_element_type=jnp.float32)
-                    gb[rows, blocks[j]] = block.astype(jnp.bfloat16)
-                    if j > i:
-                        gb[blocks[j], rows] = block.T.astype(jnp.bfloat16)
-            for i, rows in enumerate(blocks):
-                for j in range(i, len(blocks)):
-                    squared = jnp.dot(gb[rows, :], gb[:, blocks[j]],
-                                      preferred_element_type=jnp.float32)
-                    poly = (B * gb[rows, blocks[j]].astype(jnp.float32)
-                            + C * squared).astype(jnp.bfloat16)
-                    pb[rows, blocks[j]] = poly
-                    if j > i:
-                        pb[blocks[j], rows] = poly.T
+            if turn > 0:
+                for rows, others in pairs:
+                    put(rows, others, products(rows, others, slice(0, D), src))
+            for rows, others in pairs:
+                squared = jnp.dot(gb[rows, :], gb[:, others], preferred_element_type=jnp.float32)
+                poly = (B * gb[rows, others].astype(jnp.float32) + C * squared).astype(
+                    jnp.bfloat16)
+                pb[rows, others] = poly
+                if others.start > rows.start:
+                    pb[others, rows] = poly.T
             if turn < ITERS - 1:
                 for rows in strips:
                     mixed = jnp.dot(pb[rows, :], src[...], preferred_element_type=jnp.float32)
@@ -475,6 +495,7 @@
             pltpu.VMEM((tiles, OWN * EXPERTS, LANES), f32),
             pltpu.VMEM((TALL, D), bf),
             pltpu.VMEM((TALL, D), bf),
+            pltpu.VMEM((TALL, TALL), f32),
             pltpu.VMEM((TALL, TALL), bf),
             pltpu.VMEM((TALL, TALL), bf),
             pltpu.VMEM((TALL, D), bf),
@@ -494,7 +515,7 @@
             dma((2 * CHIPS,)), dma(()),
         ],
         compiler_params=pltpu.CompilerParams(
-            collective_id=0, has_side_effects=True, vmem_limit_bytes=48 * 2**20),
+            collective_id=0, has_side_effects=True, vmem_limit_bytes=209 * 2**18),
         name="muon",
     )(grads, mom)
 

time: 78.7 us -> 74.3 us (0.944)
  Pallas kernels: 74.3 us -> 70.5 us
  local copies, waits for them, and re-layouts: 3.01 us -> 1.91 us
    pallas_call x1, Pallas kernels: 74.3 us -> 70.5 us  [reduce_and_step(): pl.pallas_call(kernel, out_shape=(jax.ShapeDtypeStruct((OWN * EXPERTS, D)...]
    unnamed x4 -> x2, local copies, waits for them, and re-layouts: 2.9 us -> 1.8 us
where the time goes in v3:
time: 74.3 us; the launch traced here: 73.1 us
  Pallas kernels  70.5 us (95%)
  local copies, waits for them, and re-layouts  1.91 us (3%)
    pallas_call x1, Pallas kernels, reduce_and_step(): pl.pallas_call(kernel, out_shape=(jax.ShapeDtypeStruct((OWN * EXPERTS, D)...  70.5 us
    unnamed x2, local copies, waits for them, and re-layouts  1.8 us

profile of v3, /device:TPU:64, one launch (start us, length us, event | category | flops | bytes accessed | tf_op | source)
XLA Modules:
  0.0 73.1 jit_solution(16322574094289358491)
XLA Ops:
  0.6 70.5 %muon.1 = (f32[176,1024]{1,0:T(8,128)S(1)}, bf16[8,32,1024]{2,1,0:T(8,128)(2,1)S(1)}) custom-call(bf16[8,704,1024]{2,1,0:T(8,128)(2,1)} %bitcast.8, f32[176,1024]{1,0:T(8,128)} %bitcast.9), custom_call_target="tpu_custom_call" | custom-call | tf_op jit(solution)/shard_map/muon/pallas_call | solution.py:475
  71.2 0.1 constant_dynamic-slice_fusion
  71.3 0.9 %copy.4 = bf16[8,22,1024]{2,0,1:T(8,128)(2,1)} copy(bf16[8,22,1024]{2,1,0:T(8,128)(2,1)S(1)} %constant_dynamic-slice_fusion) | data formatting | bytes 720896
  72.3 0.9 %copy.6 = f32[8,22,1024]{2,0,1:T(8,128)} copy(f32[8,22,1024]{2,0,1:T(8,128)S(1)} %bitcast.7) | data formatting | bytes 1441792

commit v4 on v3

--- a/solution.py
+++ b/solution.py
@@ -34,7 +34,7 @@
 PART = LEFT // PARTS
 BLOCK = 256
 STRIP = 128
-EARLY = 4
+EARLY = 6
 
 
 def kernel(grads, mom, mo_out, up_out, own, got, stage, r1a, r2a, p2, r1b, r2b, r3, bl, mm, ms,
@@ -321,12 +321,10 @@
 
     def spread_all(src, base, part):
         def one(n, _):
-            @pl.when(y * SIDE * 2 + n != me)
-            def _():
-                spread(src, base, part, n).start()
-            return 0
-
-        lax.fori_loop(0, 2 * SIDE, one, 0)
+            spread(src, base, part, (2 * x + c + n) % (2 * SIDE)).start()
+            return 0
+
+        lax.fori_loop(1, 2 * SIDE, one, 0)
         rows = pl.ds(pl.multiple_of(base + SLOT * x + 16 * c, 16), 32)
         pltpu.make_async_copy(src.at[rows], up_out.at[mine, :, left(part)], u_r).start()
 

time: 74.3 us -> 74.2 us (level)
  no operation moved by 1% of the time
where the time goes in v4:
time: 74.2 us; the launch traced here: 73.2 us
  Pallas kernels  70.6 us (95%)
  local copies, waits for them, and re-layouts  1.91 us (3%)
    pallas_call x1, Pallas kernels, reduce_and_step(): pl.pallas_call(kernel, out_shape=(jax.ShapeDtypeStruct((OWN * EXPERTS, D)...  70.6 us
    unnamed x2, local copies, waits for them, and re-layouts  1.8 us

profile of v4, /device:TPU:64, one launch (start us, length us, event | category | flops | bytes accessed | tf_op | source)
XLA Modules:
  0.0 73.2 jit_solution(10276815264174870094)
XLA Ops:
  0.6 70.6 %muon.1 = (f32[176,1024]{1,0:T(8,128)S(1)}, bf16[8,32,1024]{2,1,0:T(8,128)(2,1)S(1)}) custom-call(bf16[8,704,1024]{2,1,0:T(8,128)(2,1)} %bitcast.8, f32[176,1024]{1,0:T(8,128)} %bitcast.9), custom_call_target="tpu_custom_call" | custom-call | tf_op jit(solution)/shard_map/muon/pallas_call | solution.py:473
  71.3 0.1 constant_dynamic-slice_fusion
  71.4 0.9 %copy.4 = bf16[8,22,1024]{2,0,1:T(8,128)(2,1)} copy(bf16[8,22,1024]{2,1,0:T(8,128)(2,1)S(1)} %constant_dynamic-slice_fusion) | data formatting | bytes 720896
  72.3 0.9 %copy.6 = f32[8,22,1024]{2,0,1:T(8,128)} copy(f32[8,22,1024]{2,0,1:T(8,128)S(1)} %bitcast.7) | data formatting | bytes 1441792
